TPU v7x, 256 devices: a whole 4x4x8 slice. The times are simulated.
256 devices in a mesh: gx: 16 (over z_lo, y, core), gy: 16 (over z_hi, x).
Axes of the slice: x: 4, y: 4, z: 8 (z_hi: 4, z_lo: 2; z = z_hi * 2 + z_lo), core: 2. Of those that a mesh axis runs over, the one named last changes fastest.
Arguments:
- adjoint_start: float32 [128, 128, 16, 320], P('gx', 'gy'), may hold values from -6 to 6
- source: float32 [128, 128, 16, 320], P('gx', 'gy'), may hold values from -6 to 6
- self_scale: bfloat16 [128, 128, 16, 320], P('gx', 'gy'), may hold values from 0.25 to 1.75
- relax_scale: bfloat16 [128, 128, 16, 320], P('gx', 'gy'), may hold values from 0.29882812 to 1
- face_scale: bfloat16 [6, 128, 128, 16, 320], P(None, 'gx', 'gy'), may hold values from 0.049804688 to 0.59765625
- self_block: bfloat16 [320, 320], replicated, may hold values from -0.3125 to 0.3125
- face_block: bfloat16 [6, 320, 320], replicated, may hold values from -0.3125 to 0.3125
- inverse_block: bfloat16 [320, 320], replicated, may hold values from -0.3125 to 0.3125
- shape_basis: bfloat16 [320, 128], replicated, may hold values from -0.3125 to 0.3125
- wall_elem: int32 [16, 16, 256], P('gx', 'gy'), may hold values from 0 to 1023, as said below
- wall_owner: int32 [16, 16, 256], P('gx', 'gy'), may hold values from 0 to 2048, as said below
- wall_area: float32 [16, 16, 256], P('gx', 'gy'), may hold values from 0.2 to 2
Outputs:
- adjoint: float32 [128, 128, 16, 320], P('gx', 'gy')
- patch_gradient: float32 [2048, 128], P(('gx', 'gy'))
Inputs may be any that keep to these rules, and one draw needn't show every extreme that they name: `wall_elem`: distinct local element indices within each device's tile. `wall_owner`: 2048 marks an empty slot; live slots come first in each tile; each tile has at most 256 live slots, some tile exactly 256; patch p lies in streamwise group p // (8 * 16), and in each tile at most 16 live slots name patches of one streamwise group, some tile exactly 16.
All inputs are finite; a program needn't handle non-finite values.
Results may differ from a plain program's by a relative error of at most 0.007.
Values may be sent and summed in bfloat16 or wider, within the bound.
A program may use at most 64 MiB of HBM per device.

v0:
```python
import jax
import jax.numpy as jnp
from jax import lax
from jax.sharding import PartitionSpec as P

ITERS = 2
P_DEV = 8


def padded(x, sides, width):
    for axis, dim in sides:
        size, length = (lax.axis_size(axis), x.shape[dim])
        up = [(i, (i + 1) % size) for i in range(size - 1)]
        down = [(j, i) for i, j in up]
        last = lax.slice_in_dim(x, length - width, length, axis=dim)
        initial = lax.slice_in_dim(x, 0, width, axis=dim)
        before = lax.ppermute(last, axis, up)
        after = lax.ppermute(initial, axis, down)
        x = jnp.concatenate([before, x, after], axis=dim)
    return x


def neighbours(rounded):
    padded_x = padded(rounded, (("gx", 0),), 1)
    padded_y = padded(rounded, (("gy", 1),), 1)
    lower_x = padded_x[:-2]
    upper_x = padded_x[2:]
    lower_y = padded_y[:, :-2]
    upper_y = padded_y[:, 2:]
    padded_z = jnp.pad(rounded, ((0, 0), (0, 0), (1, 1), (0, 0)))
    return [lower_x, upper_x, lower_y, upper_y, padded_z[:, :, :-2], padded_z[:, :, 2:]]


def local(
    adjoint_start,
    source,
    self_scale,
    relax_scale,
    face_scale,
    self_block,
    face_block,
    inverse_block,
    shape_basis,
    wall_elem,
    wall_owner,
    wall_area,
):
    adjoint = adjoint_start
    for step in range(ITERS):
        rounded = adjoint.astype(jnp.bfloat16)
        residual = source - self_scale * jnp.dot(
            rounded, self_block, preferred_element_type=jnp.float32
        )
        faces = neighbours(rounded)
        for face in range(6):
            residual = residual - face_scale[face] * jnp.dot(
                faces[face], face_block[face], preferred_element_type=jnp.float32
            )
        update = (relax_scale * residual).astype(jnp.bfloat16)
        adjoint = adjoint + jnp.dot(update, inverse_block, preferred_element_type=jnp.float32)
    final = adjoint.astype(jnp.bfloat16)
    width = final.shape[3]
    slots = wall_elem.shape[2]
    flat = final.reshape(-1, width)
    picked = flat[wall_elem.reshape(slots)]
    proj = jnp.dot(picked, shape_basis, preferred_element_type=jnp.float32)
    wall_row = (proj * wall_area.reshape(slots, 1)).astype(jnp.bfloat16)
    owners = wall_owner.reshape(slots)
    ids = jnp.arange(P_DEV * lax.axis_size(("gx", "gy")), dtype=jnp.int32)
    onehot = (owners[None, :] == ids[:, None]).astype(jnp.bfloat16)
    gradient = lax.psum_scatter(
        jnp.dot(onehot, wall_row, preferred_element_type=jnp.float32),
        ("gx", "gy"),
        scatter_dimension=0,
        tiled=True,
    )
    return (adjoint, gradient)


def solution(mesh):
    return jax.shard_map(
        local,
        mesh=mesh,
        in_specs=(
            P("gx", "gy", None, None),
            P("gx", "gy", None, None),
            P("gx", "gy", None, None),
            P("gx", "gy", None, None),
            P(None, "gx", "gy", None, None),
            P(),
            P(),
            P(),
            P(),
            P("gx", "gy", None),
            P("gx", "gy", None),
            P("gx", "gy", None),
        ),
        out_specs=(P("gx", "gy", None, None), P(("gx", "gy"), None)),
        check_vma=False,
    )
```

profile of v0, /device:TPU:1, one launch (start us, length us, event | category | flops | bytes accessed | tf_op | source)
XLA Modules:
  0.0 349.6 jit_solution(10738134729683002942)
XLA Ops:
  7.2 0.0 copy-start
  7.2 0.0 copy-start.2
  7.2 0.0 all-reduce.5.cloned.1.call-start
  7.2 1.6 convert_element_type.74
  8.9 5.1 %collective-permute-start.1 = (bf16[1,8,16,320]{3,2,1,0:T(8,128)(2,1)S(1)}, bf16[1,8,16,320]{3,2,1,0:T(8,128)(2,1)S(1)}, u32[]{:S(2)}, u32[]{:S(2)}) collective-permute-start(bf16[1,8,16,320]{3,2,1,0:T(8,128)(2,1)S(1)} %get-tuple-element.7), channel_id=1, source_target_pairs={{16,0},{32,16},{48,32},{64,48},{80,64},{96,80},{112,96},{128,112},... | collective-permute-start | bytes 245768 | tf_op jit(solution)/shard_map/ppermute | solution.py:18
  14.1 1.4 collective-permute-start.2
  15.5 1.3 collective-permute-start.3
  16.8 3.4 collective-permute-start
  20.2 1.8 fusion.55
  21.9 1.9 fusion.56
  23.8 1.8 fusion.101
  25.6 1.8 fusion.25
  27.4 1.8 fusion.29
  29.2 2.9 fusion.33
  32.0 9.4 %fusion.136 = (bf16[8,8,16,320]{3,2,1,0:T(8,128)(2,1)S(1)}, f32[8,8,16,320]{3,2,1,0:T(8,128)}) fusion(f32[8,8,16,320]{3,2,1,0:T(8,128)} %param.12, bf16[320,320]{1,0:T(8,128)(2,1)S(1)} %copy-done, bf16[8,8,16,320]{3,2,1,0:T(8,128)(2,1)} %param.15, f32[8,8,16,320]{3,2,1,0:T(8,128)S(1)} %copy-done.1, f32[8,8,16,320]{3,2,1,0:T(8,128)} %fusion.101, ...), kind=kOutput, calls=%fused_computation.152 | convolution fusion | flops 429424640 | bytes 21766144 | tf_op jit(solution)/shard_map/dot_general | solution.py:60
  41.4 2.9 fusion.57
  44.3 1.8 fusion.58
  46.1 1.8 fusion.99
  47.9 1.3 collective-permute-start.7
  49.2 4.9 %collective-permute-start.6 = (bf16[8,1,16,320]{3,2,1,0:T(8,128)(2,1)S(1)}, bf16[8,1,16,320]{3,2,1,0:T(8,128)(2,1)S(1)}, u32[]{:S(2)}, u32[]{:S(2)}) collective-permute-start(bf16[8,1,16,320]{3,2,1,0:T(8,128)(2,1)S(1)} %get-tuple-element.5), channel_id=1, source_target_pairs={{0,1},{1,2},{2,3},{3,4},{4,5},{5,6},{6,7},{7,8},{8,9},{9,10},{10,1... | collective-permute-start | bytes 245768 | tf_op jit(solution)/shard_map/ppermute | solution.py:17
  54.1 1.9 collective-permute-start.5
  56.0 3.8 %collective-permute-start.4 = (bf16[1,8,16,320]{3,2,1,0:T(8,128)(2,1)S(1)}, bf16[1,8,16,320]{3,2,1,0:T(8,128)(2,1)S(1)}, u32[]{:S(2)}, u32[]{:S(2)}) collective-permute-start(bf16[1,8,16,320]{3,2,1,0:T(8,128)(2,1)S(1)} %get-tuple-element.2), channel_id=1, source_target_pairs={{0,16},{16,32},{32,48},{48,64},{64,80},{80,96},{96,112},{112,128},... | collective-permute-start | bytes 245768 | tf_op jit(solution)/shard_map/ppermute | solution.py:17
  59.9 1.8 fusion.51
  61.6 1.8 fusion.47
  63.4 1.8 fusion.43
  65.2 9.3 %fusion.141 = (bf16[8,8,16,320]{3,2,1,0:T(8,128)(2,1)S(1)}, f32[8,8,16,320]{3,2,1,0:T(8,128)}) fusion(f32[8,8,16,320]{3,2,1,0:T(8,128)} %get-tuple-element.11, bf16[320,320]{1,0:T(8,128)(2,1)S(1)} %copy-done, bf16[8,8,16,320]{3,2,1,0:T(8,128)(2,1)} %param.15, f32[8,8,16,320]{3,2,1,0:T(8,128)S(1)} %copy-done.1, f32[8,8,16,320]{3,2,1,0:T(8,128)} %fusion.99, ...), kind=kOutput, calls=%fused_computation.153 | convolution fusion | flops 429424640 | bytes 21766144 | tf_op jit(solution)/shard_map/dot_general | solution.py:60
  74.6 0.0 copy-start.9
  74.6 1.2 gather_fusion
  75.8 1.6 fusion
  77.4 0.0 all-reduce.5.cloned.1.call-update
  77.4 264.1 %all-reduce.5.cloned.1.call-done = f32[2048,128]{1,0:T(8,128)} async-done(((f32[2048,128]{1,0:T(8,128)}), f32[2048,128]{1,0:T(8,128)}) %all-reduce.5.cloned.1.call-update) | async-done | bytes 1048592
  341.5 1.3 constant_dynamic-slice_fusion
  (31 shorter events, 0.2 us)
Async XLA Ops:
  7.2 24.9 %copy-start = (bf16[320,320]{1,0:T(8,128)(2,1)S(1)}, bf16[320,320]{1,0:T(8,128)(2,1)}, u32[]{:S(2)}) copy-start(bf16[320,320]{1,0:T(8,128)(2,1)} %param.19) | copy-start | bytes 614404
  7.2 13.0 %copy-start.2 = (bf16[6,320,320]{2,1,0:T(8,128)(2,1)S(1)}, bf16[6,320,320]{2,1,0:T(8,128)(2,1)}, u32[]{:S(2)}) copy-start(bf16[6,320,320]{2,1,0:T(8,128)(2,1)} %param.18) | copy-start | bytes 3686404
  7.2 334.3 %all-reduce.5.cloned.1.call-start = ((), (), s32[]{:S(2)}) async-start(), calls=%async_computation | async-start | bytes 2097152
  8.9 16.7 %collective-permute-start.1 = (bf16[1,8,16,320]{3,2,1,0:T(8,128)(2,1)S(1)}, bf16[1,8,16,320]{3,2,1,0:T(8,128)(2,1)S(1)}, u32[]{:S(2)}, u32[]{:S(2)}) collective-permute-start(bf16[1,8,16,320]{3,2,1,0:T(8,128)(2,1)S(1)} %get-tuple-element.7), channel_id=1, source_target_pairs={{16,0},{32,16},{48,32},{64,48},{80,64},{96,80},{112,96},{128,112},... | collective-permute-start | bytes 245768 | tf_op jit(solution)/shard_map/ppermute | solution.py:18
  14.1 13.3 %collective-permute-start.2 = (bf16[8,1,16,320]{3,2,1,0:T(8,128)(2,1)S(1)}, bf16[8,1,16,320]{3,2,1,0:T(8,128)(2,1)S(1)}, u32[]{:S(2)}, u32[]{:S(2)}) collective-permute-start(bf16[8,1,16,320]{3,2,1,0:T(8,128)(2,1)S(1)} %get-tuple-element.9), channel_id=1, source_target_pairs={{0,1},{1,2},{2,3},{3,4},{4,5},{5,6},{6,7},{7,8},{8,9},{9,10},{10,1... | collective-permute-start | bytes 245768 | tf_op jit(solution)/shard_map/ppermute | solution.py:17
  15.5 13.7 %collective-permute-start.3 = (bf16[8,1,16,320]{3,2,1,0:T(8,128)(2,1)S(1)}, bf16[8,1,16,320]{3,2,1,0:T(8,128)(2,1)S(1)}, u32[]{:S(2)}, u32[]{:S(2)}) collective-permute-start(bf16[8,1,16,320]{3,2,1,0:T(8,128)(2,1)S(1)} %get-tuple-element.8), channel_id=1, source_target_pairs={{1,0},{2,1},{3,2},{4,3},{5,4},{6,5},{7,6},{8,7},{9,8},{10,9},{11,1... | collective-permute-start | bytes 245768 | tf_op jit(solution)/shard_map/ppermute | solution.py:18
  16.8 15.2 %collective-permute-start = (bf16[1,8,16,320]{3,2,1,0:T(8,128)(2,1)S(1)}, bf16[1,8,16,320]{3,2,1,0:T(8,128)(2,1)S(1)}, u32[]{:S(2)}, u32[]{:S(2)}) collective-permute-start(bf16[1,8,16,320]{3,2,1,0:T(8,128)(2,1)S(1)} %get-tuple-element.6), channel_id=1, source_target_pairs={{0,16},{16,32},{32,48},{48,64},{64,80},{80,96},{96,112},{112,128},... | collective-permute-start | bytes 245768 | tf_op jit(solution)/shard_map/ppermute | solution.py:17
  21.9 1.9 copy-start.4
  23.8 1.8 copy-start.7
  29.1 2.9 copy-start.1
  41.4 2.9 copy-start.3
  44.3 1.8 copy-start.5
  47.9 12.0 %collective-permute-start.7 = (bf16[8,1,16,320]{3,2,1,0:T(8,128)(2,1)S(1)}, bf16[8,1,16,320]{3,2,1,0:T(8,128)(2,1)S(1)}, u32[]{:S(2)}, u32[]{:S(2)}) collective-permute-start(bf16[8,1,16,320]{3,2,1,0:T(8,128)(2,1)S(1)} %get-tuple-element.4), channel_id=1, source_target_pairs={{1,0},{2,1},{3,2},{4,3},{5,4},{6,5},{7,6},{8,7},{9,8},{10,9},{11,1... | collective-permute-start | bytes 245768 | tf_op jit(solution)/shard_map/ppermute | solution.py:18
  49.2 12.4 %collective-permute-start.6 = (bf16[8,1,16,320]{3,2,1,0:T(8,128)(2,1)S(1)}, bf16[8,1,16,320]{3,2,1,0:T(8,128)(2,1)S(1)}, u32[]{:S(2)}, u32[]{:S(2)}) collective-permute-start(bf16[8,1,16,320]{3,2,1,0:T(8,128)(2,1)S(1)} %get-tuple-element.5), channel_id=1, source_target_pairs={{0,1},{1,2},{2,3},{3,4},{4,5},{5,6},{6,7},{7,8},{8,9},{9,10},{10,1... | collective-permute-start | bytes 245768 | tf_op jit(solution)/shard_map/ppermute | solution.py:17
  54.1 9.3 %collective-permute-start.5 = (bf16[1,8,16,320]{3,2,1,0:T(8,128)(2,1)S(1)}, bf16[1,8,16,320]{3,2,1,0:T(8,128)(2,1)S(1)}, u32[]{:S(2)}, u32[]{:S(2)}) collective-permute-start(bf16[1,8,16,320]{3,2,1,0:T(8,128)(2,1)S(1)} %get-tuple-element.3), channel_id=1, source_target_pairs={{16,0},{32,16},{48,32},{64,48},{80,64},{96,80},{112,96},{128,112},... | collective-permute-start | bytes 245768 | tf_op jit(solution)/shard_map/ppermute | solution.py:18
  56.0 9.2 %collective-permute-start.4 = (bf16[1,8,16,320]{3,2,1,0:T(8,128)(2,1)S(1)}, bf16[1,8,16,320]{3,2,1,0:T(8,128)(2,1)S(1)}, u32[]{:S(2)}, u32[]{:S(2)}) collective-permute-start(bf16[1,8,16,320]{3,2,1,0:T(8,128)(2,1)S(1)} %get-tuple-element.2), channel_id=1, source_target_pairs={{0,16},{16,32},{32,48},{48,64},{64,80},{80,96},{96,112},{112,128},... | collective-permute-start | bytes 245768 | tf_op jit(solution)/shard_map/ppermute | solution.py:17
  74.6 1.2 copy-start.6
  74.6 1.2 copy-start.8
  74.6 1.2 copy-start.9
Sparse Core Ops, SparseCore 0:
  77.5 263.9 all-reduce.4
where the time goes:
time: 351 us; the launch traced here: 350 us
  waiting for transfers between devices  264 us (75%)
  matrix products  43.9 us (13%)
  starting transfers between devices  23.2 us (7%)
  between operations  14.2 us (4%)
    unnamed x2, waiting for transfers between devices  264 us
    dot_general x10, matrix products, local(): jnp.dot(faces[face], face_block[face], preferred_element_type=jnp.float32)  20.1 us
    dot_general x2, matrix products, local(): jnp.dot(update, inverse_block, preferred_element_type=jnp.float32)  18.7 us
    ppermute x4, starting transfers between devices, padded(): before = lax.ppermute(last, axis, up)  13.5 us
    ppermute x4, starting transfers between devices, padded(): after = lax.ppermute(initial, axis, down)  9.64 us
  transfers between devices with their start and end apart: 9, of which 1 were waited for; matrix products, arithmetic and copies ran while one was open for 5% of the time, Pallas kernels for 0%

commit v1 on v0

v1 whole, which is shorter than its diff:
```python
import functools

import jax
import jax.numpy as jnp
from jax import lax
from jax.experimental import pallas as pl
from jax.experimental.pallas import tpu as pltpu
from jax.sharding import PartitionSpec as P

ITERS = 2
P_DEV = 8
CAP = 16
MESH = pl.DeviceIdType.MESH
F32 = jnp.float32
BF16 = jnp.bfloat16


def kernel(
    nx,
    ny,
    ex,
    ey,
    ez,
    adj_hbm,
    src_hbm,
    ss_hbm,
    rx_hbm,
    fs_hbm,
    sb_hbm,
    fb_hbm,
    ib_hbm,
    basis_hbm,
    elem_hbm,
    owner_hbm,
    area_hbm,
    out_hbm,
    grad_ref,
    adj,
    src,
    ss,
    rx,
    fs,
    sb,
    fb,
    ib,
    basis,
    elem,
    owner,
    area,
    halo,
    pick,
    meta_out,
    meta_in,
    rows_out,
    rows_in,
    sums_out,
    sums_in,
    adj_sem,
    plane_sem,
    block_sem,
    wall_sem,
    out_sem,
    x_send,
    x_recv,
    y_send,
    y_recv,
    meta_send,
    meta_recv,
    rows_send,
    rows_recv,
    sums_send,
    sums_recv,
):
    gx, gy = lax.axis_index("gx"), lax.axis_index("gy")
    plane = ey * ez
    pairs = ex // 2
    width = adj.shape[2]
    group = P_DEV * ny
    slots = elem.shape[1]
    sorted_slots = nx * CAP

    adj_copies = [
        pltpu.make_async_copy(
            adj_hbm.at[pl.ds(2 * k, 2)], adj.at[pl.ds(2 * k, 2)], adj_sem.at[k]
        )
        for k in range(pairs)
    ]
    wall_copies = [
        pltpu.make_async_copy(a, b, wall_sem.at[i])
        for i, (a, b) in enumerate(
            ((elem_hbm, elem), (owner_hbm, owner), (area_hbm, area))
        )
    ]
    block_copies = [
        pltpu.make_async_copy(a, b, block_sem.at[i])
        for i, (a, b) in enumerate(
            ((sb_hbm, sb), (fb_hbm, fb), (ib_hbm, ib), (basis_hbm, basis))
        )
    ]

    def plane_copies(p, k):
        rows = pl.ds(p, 2)
        return [
            pltpu.make_async_copy(src_hbm.at[rows], src.at[rows], plane_sem.at[k, 0]),
            pltpu.make_async_copy(ss_hbm.at[rows], ss.at[rows], plane_sem.at[k, 1]),
            pltpu.make_async_copy(rx_hbm.at[rows], rx.at[rows], plane_sem.at[k, 2]),
            pltpu.make_async_copy(
                fs_hbm.at[:, rows], fs.at[:, rows], plane_sem.at[k, 3]
            ),
        ]

    order = [0, pairs - 1, *range(1, pairs - 1)]

    def place(k):
        return jnp.where(k == 0, 0, jnp.where(k == 1, pairs - 1, k - 1))

    for c in adj_copies + wall_copies + block_copies:
        c.start()
    for k, p in enumerate(order):
        for c in plane_copies(2 * p, k):
            c.start()

    if nx * ny > 1:
        barrier = pltpu.get_barrier_semaphore()

        @pl.loop(1, nx)
        def _(d):
            pl.semaphore_signal(
                barrier,
                inc=1,
                device_id=(lax.rem(gx + d, nx), gy),
                device_id_type=MESH,
            )

        @pl.loop(1, ny)
        def _(d):
            pl.semaphore_signal(
                barrier,
                inc=1,
                device_id=(gx, lax.rem(gy + d, ny)),
                device_id_type=MESH,
            )

    zx = jnp.zeros((1, plane, width), BF16)
    zy = jnp.zeros((ex, ez, width), BF16)
    for it in range(ITERS):

        @pl.when(gx == 0)
        def _():
            halo[it, 0:1, ez : ez + plane] = zx

        @pl.when(gx == nx - 1)
        def _():
            halo[it, ex + 1 : ex + 2, ez : ez + plane] = zx

        @pl.when(gy == 0)
        def _():
            halo[it, 1 : ex + 1, 0:ez] = zy

        @pl.when(gy == ny - 1)
        def _():
            halo[it, 1 : ex + 1, ez + plane : 2 * ez + plane] = zy

    for c in adj_copies:
        c.wait()
    for k in range(pairs):
        halo[0, 1 + 2 * k : 3 + 2 * k, ez : ez + plane] = adj[
            2 * k : 2 * k + 2
        ].astype(BF16)

    def x_copies(it):
        mid = pl.ds(ez, plane)
        up = pltpu.make_async_remote_copy(
            halo.at[it, ex, mid],
            halo.at[it, 0, mid],
            x_send.at[it, 0],
            x_recv.at[it, 0],
            device_id=(jnp.minimum(gx + 1, nx - 1), gy),
            device_id_type=MESH,
        )
        down = pltpu.make_async_remote_copy(
            halo.at[it, 1, mid],
            halo.at[it, ex + 1, mid],
            x_send.at[it, 1],
            x_recv.at[it, 1],
            device_id=(jnp.maximum(gx - 1, 0), gy),
            device_id_type=MESH,
        )
        return up, down

    def y_copies(it, start, count, k):
        rows = pl.ds(start + 1, count)
        up = pltpu.make_async_remote_copy(
            halo.at[it, rows, pl.ds(plane, ez)],
            halo.at[it, rows, pl.ds(0, ez)],
            y_send.at[k, 0],
            y_recv.at[k, 0],
            device_id=(gx, jnp.minimum(gy + 1, ny - 1)),
            device_id_type=MESH,
        )
        down = pltpu.make_async_remote_copy(
            halo.at[it, rows, pl.ds(ez, ez)],
            halo.at[it, rows, pl.ds(plane + ez, ez)],
            y_send.at[k, 1],
            y_recv.at[k, 1],
            device_id=(gx, jnp.maximum(gy - 1, 0)),
            device_id_type=MESH,
        )
        return up, down

    def send(pair, coord, size):
        up, down = pair

        @pl.when(coord < size - 1)
        def _():
            up.start()

        @pl.when(coord > 0)
        def _():
            down.start()

    def arrive(pair, coord, size):
        up, down = pair

        @pl.when(coord > 0)
        def _():
            up.wait_recv()

        @pl.when(coord < size - 1)
        def _():
            down.wait_recv()

    def sent(pair, coord, size):
        up, down = pair

        @pl.when(coord < size - 1)
        def _():
            up.wait_send()

        @pl.when(coord > 0)
        def _():
            down.wait_send()

    if nx * ny > 1:
        pl.semaphore_wait(barrier, nx + ny - 2)
    send(x_copies(0), gx, nx)
    send(y_copies(0, 0, ex, pairs), gy, ny)

    for c in wall_copies:
        c.wait()
    owner_row = owner[...]
    group_row = owner_row // group
    g_row = group_row.astype(F32)
    sub = lax.broadcasted_iota(jnp.int32, (slots, slots), 0)
    lane = lax.broadcasted_iota(jnp.int32, (slots, slots), 1)
    g_col = jnp.sum(jnp.where(sub == lane, g_row, 0.0), axis=1, keepdims=True)
    before = jnp.where((g_col == g_row) & (sub < lane), 1.0, 0.0)
    rank_row = jnp.sum(before, axis=0, keepdims=True)
    key_row = g_row * CAP + rank_row
    to = lax.broadcasted_iota(jnp.int32, (sorted_slots, slots), 0).astype(F32)
    perm = to == key_row
    elem_row = elem[...].astype(F32) + 1.0
    elem_col = jnp.sum(jnp.where(perm, elem_row, 0.0), axis=1, keepdims=True) - 1.0
    area_col = jnp.sum(jnp.where(perm, area[...], 0.0), axis=1, keepdims=True)
    local_row = (owner_row - group_row * group - group).astype(F32)
    local_col = jnp.sum(jnp.where(perm, local_row, 0.0), axis=1, keepdims=True) + group
    meta_out[...] = (
        jnp.broadcast_to(local_col, (sorted_slots, 128))
        .astype(BF16)
        .reshape(nx, CAP, 128)
    )
    for p in range(ex):
        at = lax.broadcasted_iota(jnp.int32, (sorted_slots, plane), 1) + p * plane
        pick[:, p * plane : (p + 1) * plane] = jnp.where(
            elem_col == at.astype(F32), 1.0, 0.0
        ).astype(BF16)

    def to_x(out, into, send_sem, recv_sem, d):
        peer = lax.rem(gx + d, nx)
        return pltpu.make_async_remote_copy(
            out.at[peer],
            into.at[gx],
            send_sem.at[d],
            recv_sem.at[d],
            device_id=(peer, gy),
            device_id_type=MESH,
        )

    def to_y(d):
        peer = lax.rem(gy + d, ny)
        return pltpu.make_async_remote_copy(
            sums_out.at[peer],
            sums_in.at[gy],
            sums_send.at[d],
            sums_recv.at[d],
            device_id=(gx, peer),
            device_id_type=MESH,
        )

    @pl.loop(1, nx)
    def _(d):
        to_x(meta_out, meta_in, meta_send, meta_recv, d).start()

    meta_in[gx] = meta_out[gx]

    for c in block_copies:
        c.wait()
    arrive(x_copies(0), gx, nx)
    arrive(y_copies(0, 0, ex, pairs), gy, ny)

    iz = lax.rem(lax.broadcasted_iota(jnp.int32, (2 * plane, width), 0), ez)

    def dot(a, b):
        return jnp.dot(a, b, preferred_element_type=F32)

    def out_copy(p, k):
        return pltpu.make_async_copy(
            adj.at[pl.ds(p, 2)], out_hbm.at[pl.ds(p, 2)], out_sem.at[k]
        )

    @pl.loop(0, ITERS * pairs)
    def _(t):
        it = t // pairs
        k = t - it * pairs
        p = 2 * place(k)

        @pl.when(it == 0)
        def _():
            for c in plane_copies(p, k):
                c.wait()

        @pl.when(it == 1)
        def _():
            arrive(y_copies(1, p, 2, k), gy, ny)

        up, down = x_copies(1)

        @pl.when((it == 1) & (k == 0) & (gx > 0))
        def _():
            up.wait_recv()

        @pl.when((it == 1) & (k == 1) & (gx < nx - 1))
        def _():
            down.wait_recv()

        def flat(x):
            return x.reshape(2 * plane, width)

        own = flat(adj[pl.ds(p, 2)])
        mid = pl.ds(ez, plane)
        zero = jnp.zeros_like(own)
        faces = [
            flat(halo[it, pl.ds(p, 2), mid]),
            flat(halo[it, pl.ds(p + 2, 2), mid]),
            flat(halo[it, pl.ds(p + 1, 2), pl.ds(0, plane)]),
            flat(halo[it, pl.ds(p + 1, 2), pl.ds(2 * ez, plane)]),
            jnp.where(iz == 0, zero, pltpu.roll(own, 1, 0)).astype(BF16),
            jnp.where(iz == ez - 1, zero, pltpu.roll(own, 2 * plane - 1, 0)).astype(
                BF16
            ),
        ]
        rows = pl.ds(p, 2)
        total = flat(src[rows]) - flat(ss[rows]).astype(F32) * dot(
            own.astype(BF16), sb[...]
        )
        for f in range(6):
            total = total - flat(fs[f, rows]).astype(F32) * dot(faces[f], fb[f])
        update = (flat(rx[rows]).astype(F32) * total).astype(BF16)
        new = (own + dot(update, ib[...])).reshape(2, plane, width)
        adj[rows] = new
        halo[it + 1, pl.ds(p + 1, 2), mid] = new.astype(BF16)

        @pl.when(it == 0)
        def _():
            send(y_copies(1, p, 2, k), gy, ny)

        @pl.when((it == 0) & (k == 1) & (gx < nx - 1))
        def _():
            up.start()

        @pl.when((it == 0) & (k == 0) & (gx > 0))
        def _():
            down.start()

        @pl.when(it == 1)
        def _():
            out_copy(p, k).start()

    picked = jnp.zeros((sorted_slots, width), F32)
    for p in range(0, ex, 2):
        picked = picked + dot(
            pick[:, p * plane : (p + 2) * plane],
            halo[ITERS, p + 1 : p + 3, ez : ez + plane].reshape(2 * plane, width),
        )
    proj = dot(picked.astype(BF16), basis[...])
    rows_out[...] = (proj * area_col).astype(BF16).reshape(nx, CAP, -1)

    @pl.loop(1, nx)
    def _(d):
        to_x(rows_out, rows_in, rows_send, rows_recv, d).start()

    rows_in[gx] = rows_out[gx]

    @pl.loop(1, nx)
    def _(d):
        to_x(meta_out, meta_in, meta_send, meta_recv, d).wait_recv()

    patch = lax.broadcasted_iota(jnp.int32, (sorted_slots, 128), 1).astype(F32)
    mark = jnp.where(
        meta_in[...].reshape(sorted_slots, 128).astype(F32) == patch, 1.0, 0.0
    ).astype(BF16)

    @pl.loop(1, nx)
    def _(d):
        to_x(rows_out, rows_in, rows_send, rows_recv, d).wait_recv()

    sums = lax.dot_general(
        mark,
        rows_in[...].reshape(sorted_slots, -1),
        (((0,), (0,)), ((), ())),
        preferred_element_type=F32,
    )
    sums_out[...] = sums[:group].reshape(ny, P_DEV, -1)

    @pl.loop(1, ny)
    def _(d):
        to_y(d).start()

    sums_in[gy] = sums_out[gy]

    @pl.loop(1, ny)
    def _(d):
        to_y(d).wait_recv()

    grad_ref[...] = jnp.sum(sums_in[...], axis=0)

    for k, p in enumerate(order):
        out_copy(2 * p, k).wait()
    for it in range(ITERS):
        sent(x_copies(it), gx, nx)
    sent(y_copies(0, 0, ex, pairs), gy, ny)
    for k, p in enumerate(order):
        sent(y_copies(1, 2 * p, 2, k), gy, ny)

    @pl.loop(1, nx)
    def _(d):
        to_x(meta_out, meta_in, meta_send, meta_recv, d).wait_send()
        to_x(rows_out, rows_in, rows_send, rows_recv, d).wait_send()

    @pl.loop(1, ny)
    def _(d):
        to_y(d).wait_send()


def local(nx, ny, adjoint, source, ss, rx, fs, sb, fb, ib, basis, elem, owner, area):
    ex, ey, ez, width = adjoint.shape
    plane, pairs = ey * ez, ex // 2
    slots = elem.shape[2]
    params = basis.shape[1]
    planes = (ex, plane, width)
    vmem, dma = pltpu.VMEM, pltpu.SemaphoreType.DMA
    anywhere = pl.BlockSpec(memory_space=pl.ANY)
    out, grad = pl.pallas_call(
        functools.partial(kernel, nx, ny, ex, ey, ez),
        out_shape=(
            jax.ShapeDtypeStruct(planes, F32),
            jax.ShapeDtypeStruct((P_DEV, params), F32),
        ),
        in_specs=[anywhere] * 12,
        out_specs=(anywhere, pl.BlockSpec(memory_space=pltpu.VMEM)),
        scratch_shapes=[
            vmem(planes, F32),
            vmem(planes, F32),
            vmem(planes, BF16),
            vmem(planes, BF16),
            vmem((6, *planes), BF16),
            vmem(sb.shape, BF16),
            vmem(fb.shape, BF16),
            vmem(ib.shape, BF16),
            vmem(basis.shape, BF16),
            vmem((1, slots), jnp.int32),
            vmem((1, slots), jnp.int32),
            vmem((1, slots), F32),
            vmem((ITERS + 1, ex + 2, plane + 2 * ez, width), BF16),
            vmem((nx * CAP, ex * plane), BF16),
            vmem((nx, CAP, 128), BF16),
            vmem((nx, CAP, 128), BF16),
            vmem((nx, CAP, params), BF16),
            vmem((nx, CAP, params), BF16),
            vmem((ny, P_DEV, params), F32),
            vmem((ny, P_DEV, params), F32),
            dma((pairs,)),
            dma((pairs, 4)),
            dma((4,)),
            dma((3,)),
            dma((pairs,)),
            dma((ITERS, 2)),
            dma((ITERS, 2)),
            dma((pairs + 1, 2)),
            dma((pairs + 1, 2)),
            dma((nx,)),
            dma((nx,)),
            dma((nx,)),
            dma((nx,)),
            dma((ny,)),
            dma((ny,)),
        ],
        compiler_params=pltpu.CompilerParams(
            collective_id=0 if nx * ny > 1 else None,
            has_side_effects=True,
            vmem_limit_bytes=62 * 1024 * 1024,
        ),
        name="sweeps",
    )(
        adjoint.reshape(planes),
        source.reshape(planes),
        ss.reshape(planes),
        rx.reshape(planes),
        fs.reshape(6, *planes),
        sb,
        fb,
        ib,
        basis,
        elem.reshape(1, slots),
        owner.reshape(1, slots),
        area.reshape(1, slots),
    )
    return out.reshape(adjoint.shape), grad


def solution(mesh):
    return jax.shard_map(
        functools.partial(local, mesh.shape["gx"], mesh.shape["gy"]),
        mesh=mesh,
        in_specs=(
            P("gx", "gy", None, None),
            P("gx", "gy", None, None),
            P("gx", "gy", None, None),
            P("gx", "gy", None, None),
            P(None, "gx", "gy", None, None),
            P(),
            P(),
            P(),
            P(),
            P("gx", "gy", None),
            P("gx", "gy", None),
            P("gx", "gy", None),
        ),
        out_specs=(P("gx", "gy", None, None), P(("gx", "gy"), None)),
        check_vma=False,
    )
```

time: 351 us -> 47.4 us (0.14)
  waiting for transfers between devices: 264 us -> 0 us
  matrix products: 43.9 us -> 0 us
  Pallas kernels: 0 us -> 43.3 us
  starting transfers between devices: 23.2 us -> 0 us
  between operations: 14.2 us -> 0.65 us
    unnamed x2 -> x0, waiting for transfers between devices: 264 us -> none
    dot_general x15 -> x0, matrix products: 43.9 us -> none  [the longest x10 20.1 us: local(): jnp.dot(faces[face], face_block[face], preferred_element_type=jnp.float32)]
    pallas_call x0 -> x1, Pallas kernels: none -> 43.3 us  [local(): pl.pallas_call(functools.partial(kernel, nx, ny, ex, ey, ez), out_shape=(...]
    ppermute x8 -> x0, starting transfers between devices: 23.1 us -> none  [the longest x4 13.5 us: padded(): before = lax.ppermute(last, axis, up)]
  transfers between devices with their start and end apart: 9 -> 0, of which waited for: 1 -> 0; matrix products, arithmetic and copies ran while one was open for 5% -> 0% of each run, Pallas kernels for 0% -> 0%
where the time goes in v1:
time: 47.4 us; the launch traced here: 47.2 us
  Pallas kernels  43.3 us (91%)
  local copies, waits for them, and re-layouts  3.27 us (7%)
  between operations  0.65 us (1%)
    pallas_call x1, Pallas kernels, local(): pl.pallas_call(functools.partial(kernel, nx, ny, ex, ey, ez), out_shape=(...  43.3 us
    unnamed x4, local copies, waits for them, and re-layouts  3.27 us

profile of v1, /device:TPU:1, one launch (start us, length us, event | category | flops | bytes accessed | tf_op | source)
XLA Modules:
  0.0 47.2 jit_solution(16656177300151340015)
XLA Ops:
  0.6 43.3 %sweeps.1 = (f32[8,128,320]{2,1,0:T(8,128)}, f32[8,128]{1,0:T(8,128)}) custom-call(f32[8,128,320]{2,1,0:T(8,128)} %bitcast.10, f32[8,128,320]{2,1,0:T(8,128)} %bitcast.11, bf16[8,128,320]{2,1,0:T(8,128)(2,1)} %bitcast.13, bf16[8,128,320]{2,1,0:T(8,128)(2,1)} %bitcast.14, bf16[6,8,128,320]{3,2,1,0:T(8,128)(2,1)} %bitcast.9, bf16[320,320]{1,0:T(8,128)(2,1)} %sb_hbm.1, ...), custom_call_target="tpu_custom_call" | custom-call | tf_op jit(solution)/shard_map/sweeps/pallas_call | solution.py:463
  44.0 0.0 copy-start
  44.0 2.7 %copy.16 = f32[8,8,16,320]{3,2,1,0:T(8,128)} copy(f32[8,8,16,320]{3,2,1,0:T(8,128)} %bitcast.12) | data formatting | bytes 2621440
  46.6 0.0 copy-done
  46.7 0.6 %copy.17 = f32[8,128]{1,0:T(8,128)} copy(f32[8,128]{1,0:T(8,128)S(1)} %copy-done) | data formatting | bytes 8192
Async XLA Ops:
  44.0 2.7 %copy-start = (f32[8,128]{1,0:T(8,128)S(1)}, f32[8,128]{1,0:T(8,128)}, u32[]{:S(2)}) copy-start(f32[8,128]{1,0:T(8,128)} %get-tuple-element.9) | copy-start | bytes 12292

commit v2 on v1

v2 whole, which is shorter than its diff:
```python
import functools

import jax
import jax.numpy as jnp
from jax import lax
from jax.experimental import pallas as pl
from jax.experimental.pallas import tpu as pltpu
from jax.sharding import PartitionSpec as P

ITERS = 2
P_DEV = 8
CAP = 16
CUTS = 2
LANES = 128
MESH = pl.DeviceIdType.MESH
F32 = jnp.float32
BF16 = jnp.bfloat16


def offsets(n, parts):
    if n != functools.reduce(lambda a, b: a * b, (size for size, _ in parts), 1):
        parts = ((n, 1),)
    steps = [()]
    for size, _ in parts:
        steps = [(*o, d) for o in steps for d in range(size)]

    def far(o):
        return sum(min(d, m - d) * hops for d, (m, hops) in zip(o, parts))

    return parts, sorted([o for o in steps if any(o)], key=lambda o: -far(o))


def peers(me, n, parts):
    parts, steps = offsets(n, parts)
    coords, rest = [], me
    for size, _ in reversed(parts):
        coords.insert(0, lax.rem(rest, size))
        rest = rest // size
    out = []
    for o in steps:
        peer = 0
        for c, d, (size, _) in zip(coords, o, parts):
            peer = peer * size + (lax.rem(c + d, size) if d else c)
        out.append(peer)
    return out


def kernel(
    nx,
    ny,
    ex,
    ey,
    ez,
    adj_hbm,
    src_hbm,
    ss_hbm,
    rx_hbm,
    fs_hbm,
    sb_hbm,
    fb_hbm,
    ib_hbm,
    basis_hbm,
    elem_hbm,
    owner_hbm,
    area_hbm,
    out_hbm,
    grad_ref,
    adj,
    src,
    ss,
    rx,
    fs,
    sb,
    fb,
    ib,
    basis,
    elem,
    owner,
    area,
    near,
    total,
    ends,
    end_out,
    x_out,
    x_halo,
    y_out,
    y_halo,
    pick,
    meta_out,
    meta_in,
    rows_out,
    rows_in,
    sums_out,
    sums_in,
    adj_sem,
    plane_sem,
    block_sem,
    wall_sem,
    out_sem,
    x_send,
    x_recv,
    y_send,
    y_recv,
    meta_send,
    meta_recv,
    rows_send,
    rows_recv,
    sums_send,
    sums_recv,
):
    gx, gy = lax.axis_index("gx"), lax.axis_index("gy")
    plane = ey * ez
    depth = ex // CUTS
    deep = depth * plane
    width = adj.shape[2]
    body = width // 256 * 256
    tail = width - body
    group = P_DEV * ny
    slots = elem.shape[1]
    sorted_slots = nx * CAP
    mid = pl.ds(ez, plane)
    x_peers = peers(gx, nx, ((2, 1), (4, 1), (2, 0.1)))
    y_peers = peers(gy, ny, ((4, 2), (4, 1)))

    low, high = pl.ds(0, ez), pl.ds(plane - ez, ez)
    inner = pl.ds(ez, plane - 2 * ez)
    adj_copies = [
        pltpu.make_async_copy(adj_hbm.at[:, a], adj.at[:, a], adj_sem.at[i])
        for i, a in enumerate((low, high, inner))
    ]
    wall_copies = [
        pltpu.make_async_copy(a, b, wall_sem.at[i])
        for i, (a, b) in enumerate(
            ((elem_hbm, elem), (owner_hbm, owner), (area_hbm, area))
        )
    ]
    block_copies = [
        pltpu.make_async_copy(a, b, block_sem.at[i])
        for i, (a, b) in enumerate(
            ((sb_hbm, sb), (fb_hbm, fb), (ib_hbm, ib), (basis_hbm, basis))
        )
    ]

    src_copy = pltpu.make_async_copy(src_hbm, src, plane_sem.at[0])
    ss_copy = pltpu.make_async_copy(ss_hbm, ss, plane_sem.at[1])
    rx_copy = pltpu.make_async_copy(rx_hbm, rx, plane_sem.at[2])
    fs_copies = [
        pltpu.make_async_copy(fs_hbm.at[f], fs.at[f], plane_sem.at[3 + f])
        for f in range(6)
    ]
    face_order = (4, 5, 0, 1, 2, 3)

    areas = (
        ((pl.ds(1, ex - 2), inner),),
        ((pl.ds(0, 1), inner), (pl.ds(ex - 1, 1), inner)),
        ((pl.ds(0, ex), low), (pl.ds(0, ex), high)),
    )

    for c in [*adj_copies, *block_copies, *wall_copies, ss_copy, src_copy]:
        c.start()

    if nx * ny > 1:
        barrier = pltpu.get_barrier_semaphore()
        for peer in x_peers:
            pl.semaphore_signal(
                barrier, inc=1, device_id=(peer, gy), device_id_type=MESH
            )
        for peer in y_peers:
            pl.semaphore_signal(
                barrier, inc=1, device_id=(gx, peer), device_id_type=MESH
            )

    zeros = jnp.zeros((ex, ez, width), BF16)
    near[0, mid] = jnp.zeros((plane, width), BF16)
    near[ex + 1, mid] = jnp.zeros((plane, width), BF16)
    near[1 : ex + 1, 0:ez] = zeros
    near[1 : ex + 1, ez + plane : 2 * ez + plane] = zeros
    end_zeros = jnp.zeros((ex, ez, 256), F32)
    end_out[0, mid, 0:256] = jnp.zeros((plane, 256), F32)
    end_out[ex + 1, mid, 0:256] = jnp.zeros((plane, 256), F32)
    end_out[1 : ex + 1, 0:ez, 0:256] = end_zeros
    end_out[1 : ex + 1, ez + plane : 2 * ez + plane, 0:256] = end_zeros
    rows_x = plane * width // LANES
    rows_y = ex * ez * width // LANES
    for it in range(ITERS):

        @pl.when(gx == 0)
        def _():
            x_halo[it, 0] = jnp.zeros((rows_x, LANES), BF16)

        @pl.when(gx == nx - 1)
        def _():
            x_halo[it, 1] = jnp.zeros((rows_x, LANES), BF16)

        @pl.when(gy == 0)
        def _():
            y_halo[it, 0] = jnp.zeros((rows_y, LANES), BF16)

        @pl.when(gy == ny - 1)
        def _():
            y_halo[it, 1] = jnp.zeros((rows_y, LANES), BF16)

    def pack(ref, x):
        n = x.shape[0]
        for j in range(body // LANES):
            ref[j * n : (j + 1) * n] = x[:, j * LANES : (j + 1) * LANES]
        end = x[:, body:width]
        ref[body // LANES * n : width * n // LANES] = jnp.concatenate(
            [end[: n // 2], end[n // 2 :]], axis=1
        )

    def unpack(ref, n):
        end = ref[body // LANES * n : width * n // LANES]
        return jnp.concatenate(
            [ref[j * n : (j + 1) * n] for j in range(body // LANES)]
            + [jnp.concatenate([end[:, 0:tail], end[:, tail : 2 * tail]], axis=0)],
            axis=1,
        )

    def sides(it, out, into, send_sem, recv_sem, ids):
        return [
            pltpu.make_async_remote_copy(
                out.at[it, i],
                into.at[it, i],
                send_sem.at[it, i],
                recv_sem.at[it, i],
                device_id=d,
                device_id_type=MESH,
            )
            for i, d in enumerate(ids)
        ]

    def x_sides(it):
        ids = ((jnp.minimum(gx + 1, nx - 1), gy), (jnp.maximum(gx - 1, 0), gy))
        return sides(it, x_out, x_halo, x_send, x_recv, ids)

    def y_sides(it):
        ids = ((gx, jnp.minimum(gy + 1, ny - 1)), (gx, jnp.maximum(gy - 1, 0)))
        return sides(it, y_out, y_halo, y_send, y_recv, ids)

    def send(it, make, me, n):
        up, down = make(it)
        pl.when(me < n - 1)(up.start)
        pl.when(me > 0)(down.start)

    def sent(it, make, me, n):
        up, down = make(it)
        pl.when(me < n - 1)(up.wait_send)
        pl.when(me > 0)(down.wait_send)

    def arrive(it, make, me, n):
        up, down = make(it)
        pl.when(me > 0)(up.wait_recv)
        pl.when(me < n - 1)(down.wait_recv)

    def send_x(it, first, final):
        pack(x_out.at[it, 0], final)
        pack(x_out.at[it, 1], first)
        send(it, x_sides, gx, nx)

    def send_y(it, first, final):
        pack(y_out.at[it, 0], final)
        pack(y_out.at[it, 1], first)
        send(it, y_sides, gy, ny)

    strip = (ex * ez, width)
    adj_copies[0].wait()
    adj_copies[1].wait()
    if nx * ny > 1:
        pl.semaphore_wait(barrier, nx + ny - 2)
    send_y(
        0,
        adj[:, low].astype(BF16).reshape(strip),
        adj[:, high].astype(BF16).reshape(strip),
    )
    adj_copies[2].wait()
    send_x(0, adj[0].astype(BF16), adj[ex - 1].astype(BF16))
    for c in [fs_copies[4], fs_copies[5], fs_copies[0]]:
        c.start()
    for k in range(CUTS):
        near[1 + depth * k : 1 + depth * (k + 1), mid] = adj[
            depth * k : depth * (k + 1)
        ].astype(BF16)

    for c in wall_copies:
        c.wait()
    owner_row = owner[...]
    group_row = owner_row // group
    g_row = group_row.astype(F32)
    sub = lax.broadcasted_iota(jnp.int32, (slots, slots), 0)
    lane = lax.broadcasted_iota(jnp.int32, (slots, slots), 1)
    g_col = jnp.sum(jnp.where(sub == lane, g_row, 0.0), axis=1, keepdims=True)
    before = jnp.where((g_col == g_row) & (sub < lane), 1.0, 0.0)
    rank_row = jnp.sum(before, axis=0, keepdims=True)
    key_row = g_row * CAP + rank_row
    to = lax.broadcasted_iota(jnp.int32, (sorted_slots, slots), 0).astype(F32)
    perm = to == key_row
    local_row = (owner_row - group_row * group - group).astype(F32)
    local_col = jnp.sum(jnp.where(perm, local_row, 0.0), axis=1, keepdims=True) + group
    meta_out[...] = (
        jnp.broadcast_to(local_col, (sorted_slots, LANES))
        .astype(BF16)
        .reshape(nx, CAP, LANES)
    )
    elem_row = elem[...].astype(F32) + 1.0
    elem_col = jnp.sum(jnp.where(perm, elem_row, 0.0), axis=1, keepdims=True) - 1.0
    area_col = jnp.sum(jnp.where(perm, area[...], 0.0), axis=1, keepdims=True)
    for p in range(ex):
        at = lax.broadcasted_iota(jnp.int32, (sorted_slots, plane), 1) + p * plane
        pick[:, p * plane : (p + 1) * plane] = jnp.where(
            elem_col == at.astype(F32), 1.0, 0.0
        ).astype(BF16)

    def to_x(out, into, send_sem, recv_sem):
        return [
            pltpu.make_async_remote_copy(
                out.at[peer],
                into.at[gx],
                send_sem,
                recv_sem,
                device_id=(peer, gy),
                device_id_type=MESH,
            )
            for peer in x_peers
        ]

    def to_y():
        return [
            pltpu.make_async_remote_copy(
                sums_out.at[peer],
                sums_in.at[gy],
                sums_send,
                sums_recv,
                device_id=(gx, peer),
                device_id_type=MESH,
            )
            for peer in y_peers
        ]

    def wait_all(ref, n, sem):
        if n > 1:
            block = ref.at[pl.ds(0, n - 1)]
            pltpu.make_async_copy(block, block, sem).wait()

    for c in to_x(meta_out, meta_in, meta_send, meta_recv):
        c.start()
    meta_in[gx] = meta_out[gx]

    for c in block_copies:
        c.wait()
    last = [fb[f, :, body:width] for f in range(4)] + [
        sb[:, body:width],
        fb[4, :, body:width],
        fb[5, :, body:width],
        jnp.zeros((width, tail), BF16),
    ]
    for j in range(4):
        ends[:, j * LANES : (j + 1) * LANES] = jnp.concatenate(
            last[2 * j : 2 * j + 2], axis=1
        )

    iz = lax.rem(lax.broadcasted_iota(jnp.int32, (deep, 1), 0), ez)
    first_z, last_z = iz == 0, iz == ez - 1

    def dot(a, b):
        return jnp.dot(a, b, preferred_element_type=F32)

    def flat(x):
        return x.reshape(deep, x.shape[-1])

    def below(x):
        return jnp.where(first_z, 0.0, pltpu.roll(x, 1, 0))

    def above(x):
        return jnp.where(last_z, 0.0, pltpu.roll(x, deep - 1, 0))

    for it in range(ITERS):
        for k in range(CUTS):
            end_out[k * depth + 1 : k * depth + 1 + depth, mid] = dot(
                flat(near[k * depth + 1 : k * depth + 1 + depth, mid]), ends[...]
            ).reshape(depth, plane, 4 * LANES)

        if it == 0:
            ss_copy.wait()
            src_copy.wait()
        for k in range(CUTS):
            rows = pl.ds(k * depth, depth)
            here = (pl.ds(k * depth + 1, depth), mid)
            two = flat(end_out[(*here, slice(2 * LANES, 3 * LANES))])
            total[rows, :, 0:body] = src[rows, :, 0:body] - ss[rows, :, 0:body].astype(
                F32
            ) * dot(flat(near[here]), sb[:, 0:body]).reshape(depth, plane, body)
            total[rows, :, body:width] = src[rows, :, body:width] - ss[
                rows, :, body:width
            ].astype(F32) * two[:, 0:tail].reshape(depth, plane, tail)
        if it == 0:
            for c in [fs_copies[1], fs_copies[2], fs_copies[3], rx_copy]:
                c.start()
        for f in face_order:
            if it == 0:
                fs_copies[f].wait()
            for k in range(CUTS):
                p = k * depth
                rows = pl.ds(p, depth)
                if f < 4:
                    place = (
                        (pl.ds(p, depth), mid),
                        (pl.ds(p + 2, depth), mid),
                        (pl.ds(p + 1, depth), pl.ds(0, plane)),
                        (pl.ds(p + 1, depth), pl.ds(2 * ez, plane)),
                    )[f]
                    face = flat(near[place])
                    j = f // 2
                    end = flat(end_out[(*place, slice(j * LANES, (j + 1) * LANES))])
                    end = end[:, 0:tail] if f % 2 == 0 else end[:, tail : 2 * tail]
                else:
                    shift = below if f == 4 else above
                    face = shift(flat(adj[rows])).astype(BF16)
                    j = f - 2
                    end = shift(
                        flat(
                            end_out[
                                p + 1 : p + 1 + depth,
                                mid,
                                j * LANES : (j + 1) * LANES,
                            ]
                        )
                    )
                    end = end[:, tail : 2 * tail] if f == 4 else end[:, 0:tail]
                total[rows, :, 0:body] -= fs[f, rows, :, 0:body].astype(F32) * dot(
                    face, fb[f, :, 0:body]
                ).reshape(depth, plane, body)
                total[rows, :, body:width] -= fs[f, rows, :, body:width].astype(
                    F32
                ) * end.reshape(depth, plane, tail)

        if it == 0:
            rx_copy.wait()

        def renew(area):
            update = [
                (rx[a].astype(F32) * total[a]).astype(BF16).reshape(-1, width)
                for a in area
            ]
            step = dot(jnp.concatenate(update, axis=0), ib[...])
            start = 0
            for a, u in zip(area, update):
                new = adj[a] + step[start : start + u.shape[0]].reshape(adj[a].shape)
                start += u.shape[0]
                adj[a] = new
                rows, columns = a
                near[
                    pl.ds(rows.start + 1, rows.size),
                    pl.ds(columns.start + ez, columns.size),
                ] = new.astype(BF16)

        renew(areas[0])
        arrive(it, x_sides, gx, nx)
        for side, p in enumerate((0, ex - 1)):
            total[p] = total[p] - fs[side, p].astype(F32) * dot(
                unpack(x_halo.at[it, side], plane), fb[side]
            )
        renew(areas[1])
        arrive(it, y_sides, gy, ny)
        for side, a in enumerate((low, high)):
            total[:, a] = total[:, a] - fs[2 + side, :, a].astype(F32) * dot(
                unpack(y_halo.at[it, side], ex * ez), fb[2 + side]
            ).reshape(ex, ez, width)
        renew(areas[2])
        if it < ITERS - 1:
            send_y(
                it + 1,
                near[1 : ex + 1, pl.ds(ez, ez)].reshape(strip),
                near[1 : ex + 1, pl.ds(plane, ez)].reshape(strip),
            )
            send_x(it + 1, near[1, mid], near[ex, mid])

    out_copy = pltpu.make_async_copy(adj, out_hbm, out_sem.at[0])
    out_copy.start()

    picked = jnp.zeros((sorted_slots, width), F32)
    for k in range(CUTS):
        picked = picked + dot(
            pick[:, k * deep : (k + 1) * deep],
            flat(near[1 + depth * k : 1 + depth * (k + 1), mid]),
        )
    proj = dot(picked.astype(BF16), basis[...])
    rows_out[...] = (proj * area_col).astype(BF16).reshape(nx, CAP, -1)
    for c in to_x(rows_out, rows_in, rows_send, rows_recv):
        c.start()
    rows_in[gx] = rows_out[gx]

    wait_all(meta_in, nx, meta_recv)
    patch = lax.broadcasted_iota(jnp.int32, (sorted_slots, LANES), 1).astype(F32)
    mark = jnp.where(
        meta_in[...].reshape(sorted_slots, LANES).astype(F32) == patch, 1.0, 0.0
    ).astype(BF16)
    wait_all(rows_in, nx, rows_recv)
    sums = lax.dot_general(
        mark,
        rows_in[...].reshape(sorted_slots, -1),
        (((0,), (0,)), ((), ())),
        preferred_element_type=F32,
    )
    sums_out[...] = sums[:group].reshape(ny, P_DEV, -1)
    for c in to_y():
        c.start()
    sums_in[gy] = sums_out[gy]

    out_copy.wait()
    for it in range(ITERS):
        sent(it, x_sides, gx, nx)
        sent(it, y_sides, gy, ny)
    wait_all(meta_out, nx, meta_send)
    wait_all(rows_out, nx, rows_send)
    wait_all(sums_out, ny, sums_send)
    wait_all(sums_in, ny, sums_recv)
    grad_ref[...] = jnp.sum(sums_in[...], axis=0)


def store(out, grad, out_hbm, grad_hbm, held, held_grad, in_sem, out_sem):
    parts = in_sem.shape[0] - 1
    size = out.shape[0] // parts
    cuts = [pl.ds(k * size, size) for k in range(parts)]
    into = [
        pltpu.make_async_copy(out.at[r], held.at[r], in_sem.at[k])
        for k, r in enumerate(cuts)
    ] + [pltpu.make_async_copy(grad, held_grad, in_sem.at[parts])]
    away = [
        pltpu.make_async_copy(held.at[r], out_hbm.at[r], out_sem.at[k])
        for k, r in enumerate(cuts)
    ] + [pltpu.make_async_copy(held_grad, grad_hbm, out_sem.at[parts])]
    for c in into:
        c.start()
    for c, d in zip(into, away):
        c.wait()
        d.start()
    for d in away:
        d.wait()


def local(nx, ny, adjoint, source, ss, rx, fs, sb, fb, ib, basis, elem, owner, area):
    ex, ey, ez, width = adjoint.shape
    plane = ey * ez
    slots = elem.shape[2]
    params = basis.shape[1]
    planes = (ex, plane, width)
    vmem, dma = pltpu.VMEM, pltpu.SemaphoreType.DMA
    anywhere = pl.BlockSpec(memory_space=pl.ANY)
    out, grad = pl.pallas_call(
        functools.partial(kernel, nx, ny, ex, ey, ez),
        out_shape=(
            jax.ShapeDtypeStruct(planes, F32),
            jax.ShapeDtypeStruct((P_DEV, params), F32),
        ),
        in_specs=[anywhere] * 12,
        out_specs=(anywhere, pl.BlockSpec(memory_space=pltpu.VMEM)),
        scratch_shapes=[
            vmem(planes, F32),
            vmem(planes, F32),
            vmem(planes, BF16),
            vmem(planes, BF16),
            vmem((6, *planes), BF16),
            vmem(sb.shape, BF16),
            vmem(fb.shape, BF16),
            vmem(ib.shape, BF16),
            vmem(basis.shape, BF16),
            vmem((1, slots), jnp.int32),
            vmem((1, slots), jnp.int32),
            vmem((1, slots), F32),
            vmem((ex + 2, plane + 2 * ez, width), BF16),
            vmem(planes, F32),
            vmem((width, 4 * LANES), BF16),
            vmem((ex + 2, plane + 2 * ez, 4 * LANES), F32),
            vmem((ITERS, 2, plane * width // LANES, LANES), BF16),
            vmem((ITERS, 2, plane * width // LANES, LANES), BF16),
            vmem((ITERS, 2, ex * ez * width // LANES, LANES), BF16),
            vmem((ITERS, 2, ex * ez * width // LANES, LANES), BF16),
            vmem((nx * CAP, ex * plane), BF16),
            vmem((nx, CAP, LANES), BF16),
            vmem((nx, CAP, LANES), BF16),
            vmem((nx, CAP, params), BF16),
            vmem((nx, CAP, params), BF16),
            vmem((ny, P_DEV, params), F32),
            vmem((ny, P_DEV, params), F32),
            dma((3,)),
            dma((9,)),
            dma((4,)),
            dma((3,)),
            dma((3,)),
            dma((ITERS, 2)),
            dma((ITERS, 2)),
            dma((ITERS, 2)),
            dma((ITERS, 2)),
            dma,
            dma,
            dma,
            dma,
            dma,
            dma,
        ],
        compiler_params=pltpu.CompilerParams(
            collective_id=0 if nx * ny > 1 else None,
            has_side_effects=True,
            vmem_limit_bytes=62 * 1024 * 1024,
        ),
        name="sweeps",
    )(
        adjoint.reshape(planes),
        source.reshape(planes),
        ss.reshape(planes),
        rx.reshape(planes),
        fs.reshape(6, *planes),
        sb,
        fb,
        ib,
        basis,
        elem.reshape(1, slots),
        owner.reshape(1, slots),
        area.reshape(1, slots),
    )
    hbm = pl.BlockSpec(memory_space=pltpu.HBM)
    out, grad = pl.pallas_call(
        store,
        out_shape=(
            jax.ShapeDtypeStruct(planes, F32),
            jax.ShapeDtypeStruct((P_DEV, params), F32),
        ),
        in_specs=[anywhere] * 2,
        out_specs=(hbm, hbm),
        scratch_shapes=[
            vmem(planes, F32),
            vmem(grad.shape, F32),
            dma((5,)),
            dma((5,)),
        ],
        name="store",
    )(out, grad)
    return out.reshape(adjoint.shape), grad


def solution(mesh):
    return jax.shard_map(
        functools.partial(local, mesh.shape["gx"], mesh.shape["gy"]),
        mesh=mesh,
        in_specs=(
            P("gx", "gy", None, None),
            P("gx", "gy", None, None),
            P("gx", "gy", None, None),
            P("gx", "gy", None, None),
            P(None, "gx", "gy", None, None),
            P(),
            P(),
            P(),
            P(),
            P("gx", "gy", None),
            P("gx", "gy", None),
            P("gx", "gy", None),
        ),
        out_specs=(P("gx", "gy", None, None), P(("gx", "gy"), None)),
        check_vma=False,
    )
```

time: 47.4 us -> 38.9 us (0.82)
  Pallas kernels: 43.3 us -> 38.1 us
  local copies, waits for them, and re-layouts: 3.27 us -> 0 us
    pallas_call x1, Pallas kernels: 43.3 us -> 35.9 us  [local(): pl.pallas_call(functools.partial(kernel, nx, ny, ex, ey, ez), out_shape=(...]
    unnamed x4 -> x0, local copies, waits for them, and re-layouts: 3.27 us -> none
    pallas_call x0 -> x1, Pallas kernels: none -> 2.22 us  [local(): pl.pallas_call(store, out_shape=(jax.ShapeDtypeStruct(planes, F32), jax.S...]
where the time goes in v2:
time: 38.9 us; the launch traced here: 38.8 us
  Pallas kernels  38.1 us (98%)
  between operations  0.64 us (2%)
    pallas_call x1, Pallas kernels, local(): pl.pallas_call(functools.partial(kernel, nx, ny, ex, ey, ez), out_shape=(...  35.9 us
    pallas_call x1, Pallas kernels, local(): pl.pallas_call(store, out_shape=(jax.ShapeDtypeStruct(planes, F32), jax.S...  2.22 us

profile of v2, /device:TPU:1, one launch (start us, length us, event | category | flops | bytes accessed | tf_op | source)
XLA Modules:
  0.0 38.8 jit_solution(18358026694388270586)
XLA Ops:
  0.6 35.9 %sweeps.1 = (f32[8,128,320]{2,1,0:T(8,128)}, f32[8,128]{1,0:T(8,128)}) custom-call(f32[8,128,320]{2,1,0:T(8,128)} %bitcast.10, f32[8,128,320]{2,1,0:T(8,128)} %bitcast.11, bf16[8,128,320]{2,1,0:T(8,128)(2,1)} %bitcast.12, bf16[8,128,320]{2,1,0:T(8,128)(2,1)} %bitcast.13, bf16[6,8,128,320]{3,2,1,0:T(8,128)(2,1)} %bitcast.9, bf16[320,320]{1,0:T(8,128)(2,1)} %sb_hbm.1, ...), custom_call_target="tpu_custom_call" | custom-call | tf_op jit(solution)/shard_map/sweeps/pallas_call | solution.py:550
  36.6 2.2 %store.1 = (f32[8,128,320]{2,1,0:T(8,128)}, f32[8,128]{1,0:T(8,128)}) custom-call(f32[8,128,320]{2,1,0:T(8,128)} %get-tuple-element.6.out, f32[8,128]{1,0:T(8,128)} %get-tuple-element.7.grad), custom_call_target="tpu_custom_call" | custom-call | tf_op jit(solution)/shard_map/store/pallas_call | solution.py:623

commit v3 on v2

--- a/solution.py
+++ b/solution.py
@@ -63,9 +63,8 @@
     elem_hbm,
     owner_hbm,
     area_hbm,
-    out_hbm,
+    adj,
     grad_ref,
-    adj,
     src,
     ss,
     rx,
@@ -96,7 +95,6 @@
     plane_sem,
     block_sem,
     wall_sem,
-    out_sem,
     x_send,
     x_recv,
     y_send,
@@ -475,9 +473,6 @@
             )
             send_x(it + 1, near[1, mid], near[ex, mid])
 
-    out_copy = pltpu.make_async_copy(adj, out_hbm, out_sem.at[0])
-    out_copy.start()
-
     picked = jnp.zeros((sorted_slots, width), F32)
     for k in range(CUTS):
         picked = picked + dot(
@@ -507,7 +502,6 @@
         c.start()
     sums_in[gy] = sums_out[gy]
 
-    out_copy.wait()
     for it in range(ITERS):
         sent(it, x_sides, gx, nx)
         sent(it, y_sides, gy, ny)
@@ -518,25 +512,15 @@
     grad_ref[...] = jnp.sum(sums_in[...], axis=0)
 
 
-def store(out, grad, out_hbm, grad_hbm, held, held_grad, in_sem, out_sem):
-    parts = in_sem.shape[0] - 1
-    size = out.shape[0] // parts
-    cuts = [pl.ds(k * size, size) for k in range(parts)]
-    into = [
-        pltpu.make_async_copy(out.at[r], held.at[r], in_sem.at[k])
-        for k, r in enumerate(cuts)
-    ] + [pltpu.make_async_copy(grad, held_grad, in_sem.at[parts])]
-    away = [
-        pltpu.make_async_copy(held.at[r], out_hbm.at[r], out_sem.at[k])
-        for k, r in enumerate(cuts)
-    ] + [pltpu.make_async_copy(held_grad, grad_hbm, out_sem.at[parts])]
-    for c in into:
+def store(out, grad, out_hbm, grad_hbm, sem):
+    copies = [
+        pltpu.make_async_copy(a, b, sem.at[i])
+        for i, (a, b) in enumerate(((out, out_hbm), (grad, grad_hbm)))
+    ]
+    for c in copies:
         c.start()
-    for c, d in zip(into, away):
+    for c in copies:
         c.wait()
-        d.start()
-    for d in away:
-        d.wait()
 
 
 def local(nx, ny, adjoint, source, ss, rx, fs, sb, fb, ib, basis, elem, owner, area):
@@ -549,14 +533,10 @@
     anywhere = pl.BlockSpec(memory_space=pl.ANY)
     out, grad = pl.pallas_call(
         functools.partial(kernel, nx, ny, ex, ey, ez),
-        out_shape=(
-            jax.ShapeDtypeStruct(planes, F32),
-            jax.ShapeDtypeStruct((P_DEV, params), F32),
-        ),
+        out_shape=(vmem(planes, F32), vmem((P_DEV, params), F32)),
         in_specs=[anywhere] * 12,
-        out_specs=(anywhere, pl.BlockSpec(memory_space=pltpu.VMEM)),
+        out_specs=(pl.BlockSpec(memory_space=pltpu.VMEM),) * 2,
         scratch_shapes=[
-            vmem(planes, F32),
             vmem(planes, F32),
             vmem(planes, BF16),
             vmem(planes, BF16),
@@ -587,7 +567,6 @@
             dma((9,)),
             dma((4,)),
             dma((3,)),
-            dma((3,)),
             dma((ITERS, 2)),
             dma((ITERS, 2)),
             dma((ITERS, 2)),
@@ -602,7 +581,7 @@
         compiler_params=pltpu.CompilerParams(
             collective_id=0 if nx * ny > 1 else None,
             has_side_effects=True,
-            vmem_limit_bytes=62 * 1024 * 1024,
+            vmem_limit_bytes=62_000_000,
         ),
         name="sweeps",
     )(
@@ -626,14 +605,10 @@
             jax.ShapeDtypeStruct(planes, F32),
             jax.ShapeDtypeStruct((P_DEV, params), F32),
         ),
-        in_specs=[anywhere] * 2,
+        in_specs=[pl.BlockSpec(memory_space=pltpu.VMEM)] * 2,
         out_specs=(hbm, hbm),
-        scratch_shapes=[
-            vmem(planes, F32),
-            vmem(grad.shape, F32),
-            dma((5,)),
-            dma((5,)),
-        ],
+        scratch_shapes=[dma((2,))],
+        compiler_params=pltpu.CompilerParams(vmem_limit_bytes=8 * 1024 * 1024),
         name="store",
     )(out, grad)
     return out.reshape(adjoint.shape), grad

time: 38.9 us -> 37.1 us (0.954)
  Pallas kernels: 38.1 us -> 36.3 us
    pallas_call x1, Pallas kernels: 2.22 us -> 1.16 us  [local(): pl.pallas_call(store, out_shape=(jax.ShapeDtypeStruct(planes, F32), jax.S...]
    pallas_call x1, Pallas kernels: 35.9 us -> 35.2 us  [local(): pl.pallas_call(functools.partial(kernel, nx, ny, ex, ey, ez), out_shape=(...]
where the time goes in v3:
time: 37.1 us; the launch traced here: 37 us
  Pallas kernels  36.3 us (98%)
  between operations  0.64 us (2%)
    pallas_call x1, Pallas kernels, local(): pl.pallas_call(functools.partial(kernel, nx, ny, ex, ey, ez), out_shape=(...  35.2 us
    pallas_call x1, Pallas kernels, local(): pl.pallas_call(store, out_shape=(jax.ShapeDtypeStruct(planes, F32), jax.S...  1.16 us

profile of v3, /device:TPU:1, one launch (start us, length us, event | category | flops | bytes accessed | tf_op | source)
XLA Modules:
  0.0 37.0 jit_solution(6278821347232319036)
XLA Ops:
  0.6 35.2 %sweeps.1 = (f32[8,128,320]{2,1,0:T(8,128)S(1)}, f32[8,128]{1,0:T(8,128)S(1)}) custom-call(f32[8,128,320]{2,1,0:T(8,128)} %bitcast.10, f32[8,128,320]{2,1,0:T(8,128)} %bitcast.11, bf16[8,128,320]{2,1,0:T(8,128)(2,1)} %bitcast.12, bf16[8,128,320]{2,1,0:T(8,128)(2,1)} %bitcast.13, bf16[6,8,128,320]{3,2,1,0:T(8,128)(2,1)} %bitcast.9, bf16[320,320]{1,0:T(8,128)(2,1)} %sb_hbm.1, ...), custom_call_target="tpu_custom_call" | custom-call | tf_op jit(solution)/shard_map/sweeps/pallas_call | solution.py:534
  35.8 1.2 %store.1 = (f32[8,128,320]{2,1,0:T(8,128)}, f32[8,128]{1,0:T(8,128)}) custom-call(f32[8,128,320]{2,1,0:T(8,128)S(1)} %get-tuple-element.6.out, f32[8,128]{1,0:T(8,128)S(1)} %get-tuple-element.7.grad), custom_call_target="tpu_custom_call" | custom-call | tf_op jit(solution)/shard_map/store/pallas_call | solution.py:602

commit v4 on v3

--- a/solution.py
+++ b/solution.py
@@ -85,6 +85,7 @@
     y_out,
     y_halo,
     pick,
+    mark,
     meta_out,
     meta_in,
     rows_out,
@@ -257,9 +258,11 @@
         send(it, x_sides, gx, nx)
 
     def send_y(it, first, final):
+        up, down = y_sides(it)
         pack(y_out.at[it, 0], final)
+        pl.when(gy < ny - 1)(up.start)
         pack(y_out.at[it, 1], first)
-        send(it, y_sides, gy, ny)
+        pl.when(gy > 0)(down.start)
 
     strip = (ex * ez, width)
     adj_copies[0].wait()
@@ -275,6 +278,7 @@
     send_x(0, adj[0].astype(BF16), adj[ex - 1].astype(BF16))
     for c in [fs_copies[4], fs_copies[5], fs_copies[0]]:
         c.start()
+
     for k in range(CUTS):
         near[1 + depth * k : 1 + depth * (k + 1), mid] = adj[
             depth * k : depth * (k + 1)
@@ -303,11 +307,14 @@
     elem_row = elem[...].astype(F32) + 1.0
     elem_col = jnp.sum(jnp.where(perm, elem_row, 0.0), axis=1, keepdims=True) - 1.0
     area_col = jnp.sum(jnp.where(perm, area[...], 0.0), axis=1, keepdims=True)
-    for p in range(ex):
-        at = lax.broadcasted_iota(jnp.int32, (sorted_slots, plane), 1) + p * plane
-        pick[:, p * plane : (p + 1) * plane] = jnp.where(
-            elem_col == at.astype(F32), 1.0, 0.0
-        ).astype(BF16)
+    most = plane - 2 * ez
+    column = lax.broadcasted_iota(jnp.int32, (1, ex * plane), 1)
+    on = column - ex * most
+    off_at = column // most * plane + ez + lax.rem(column, most)
+    on_low = on // ez * plane + lax.rem(on, ez)
+    on_high = (on - ex * ez) // ez * plane + plane - ez + lax.rem(on, ez)
+    at = jnp.where(on < 0, off_at, jnp.where(on < ex * ez, on_low, on_high))
+    pick[...] = jnp.where(elem_col == at.astype(F32), 1.0, 0.0).astype(BF16)
 
     def to_x(out, into, send_sem, recv_sem):
         return [
@@ -459,6 +466,11 @@
                 unpack(x_halo.at[it, side], plane), fb[side]
             )
         renew(areas[1])
+        if it == ITERS - 1:
+            picked = dot(
+                pick[:, 0 : ex * most],
+                near[1 : ex + 1, pl.ds(2 * ez, most)].reshape(-1, width),
+            )
         arrive(it, y_sides, gy, ny)
         for side, a in enumerate((low, high)):
             total[:, a] = total[:, a] - fs[2 + side, :, a].astype(F32) * dot(
@@ -473,11 +485,10 @@
             )
             send_x(it + 1, near[1, mid], near[ex, mid])
 
-    picked = jnp.zeros((sorted_slots, width), F32)
-    for k in range(CUTS):
+    for i, a in enumerate((pl.ds(ez, ez), pl.ds(plane, ez))):
+        start = ex * (most + i * ez)
         picked = picked + dot(
-            pick[:, k * deep : (k + 1) * deep],
-            flat(near[1 + depth * k : 1 + depth * (k + 1), mid]),
+            pick[:, start : start + ex * ez], near[1 : ex + 1, a].reshape(strip)
         )
     proj = dot(picked.astype(BF16), basis[...])
     rows_out[...] = (proj * area_col).astype(BF16).reshape(nx, CAP, -1)
@@ -487,16 +498,11 @@
 
     wait_all(meta_in, nx, meta_recv)
     patch = lax.broadcasted_iota(jnp.int32, (sorted_slots, LANES), 1).astype(F32)
-    mark = jnp.where(
+    mark[...] = jnp.where(
         meta_in[...].reshape(sorted_slots, LANES).astype(F32) == patch, 1.0, 0.0
-    ).astype(BF16)
+    ).T.astype(BF16)
     wait_all(rows_in, nx, rows_recv)
-    sums = lax.dot_general(
-        mark,
-        rows_in[...].reshape(sorted_slots, -1),
-        (((0,), (0,)), ((), ())),
-        preferred_element_type=F32,
-    )
+    sums = dot(mark[...], rows_in[...].reshape(sorted_slots, -1))
     sums_out[...] = sums[:group].reshape(ny, P_DEV, -1)
     for c in to_y():
         c.start()
@@ -513,9 +519,9 @@
 
 
 def store(out, grad, out_hbm, grad_hbm, sem):
-    copies = [
-        pltpu.make_async_copy(a, b, sem.at[i])
-        for i, (a, b) in enumerate(((out, out_hbm), (grad, grad_hbm)))
+    copies = [pltpu.make_async_copy(grad, grad_hbm, sem.at[out.shape[0]])] + [
+        pltpu.make_async_copy(out.at[p], out_hbm.at[p], sem.at[p])
+        for p in range(out.shape[0])
     ]
     for c in copies:
         c.start()
@@ -557,6 +563,7 @@
             vmem((ITERS, 2, ex * ez * width // LANES, LANES), BF16),
             vmem((ITERS, 2, ex * ez * width // LANES, LANES), BF16),
             vmem((nx * CAP, ex * plane), BF16),
+            vmem((LANES, nx * CAP), BF16),
             vmem((nx, CAP, LANES), BF16),
             vmem((nx, CAP, LANES), BF16),
             vmem((nx, CAP, params), BF16),
@@ -607,7 +614,7 @@
         ),
         in_specs=[pl.BlockSpec(memory_space=pltpu.VMEM)] * 2,
         out_specs=(hbm, hbm),
-        scratch_shapes=[dma((2,))],
+        scratch_shapes=[dma((ex + 1,))],
         compiler_params=pltpu.CompilerParams(vmem_limit_bytes=8 * 1024 * 1024),
         name="store",
     )(out, grad)

time: 37.1 us -> 37.1 us (level)
  no operation moved by 1% of the time
where the time goes in v4:
time: 37.1 us; the launch traced here: 37 us
  Pallas kernels  36.4 us (98%)
  between operations  0.64 us (2%)
    pallas_call x1, Pallas kernels, local(): pl.pallas_call(functools.partial(kernel, nx, ny, ex, ey, ez), out_shape=(...  35.2 us
    pallas_call x1, Pallas kernels, local(): pl.pallas_call(store, out_shape=(jax.ShapeDtypeStruct(planes, F32), jax.S...  1.21 us

profile of v4, /device:TPU:1, one launch (start us, length us, event | category | flops | bytes accessed | tf_op | source)
XLA Modules:
  0.0 37.0 jit_solution(12843478117764463748)
XLA Ops:
  0.6 35.2 %sweeps.1 = (f32[8,128,320]{2,1,0:T(8,128)S(1)}, f32[8,128]{1,0:T(8,128)S(1)}) custom-call(f32[8,128,320]{2,1,0:T(8,128)} %bitcast.10, f32[8,128,320]{2,1,0:T(8,128)} %bitcast.11, bf16[8,128,320]{2,1,0:T(8,128)(2,1)} %bitcast.12, bf16[8,128,320]{2,1,0:T(8,128)(2,1)} %bitcast.13, bf16[6,8,128,320]{3,2,1,0:T(8,128)(2,1)} %bitcast.9, bf16[320,320]{1,0:T(8,128)(2,1)} %sb_hbm.1, ...), custom_call_target="tpu_custom_call" | custom-call | tf_op jit(solution)/shard_map/sweeps/pallas_call | solution.py:540
  35.8 1.2 %store.1 = (f32[8,128,320]{2,1,0:T(8,128)}, f32[8,128]{1,0:T(8,128)}) custom-call(f32[8,128,320]{2,1,0:T(8,128)S(1)} %get-tuple-element.6.out, f32[8,128]{1,0:T(8,128)S(1)} %get-tuple-element.7.grad), custom_call_target="tpu_custom_call" | custom-call | tf_op jit(solution)/shard_map/store/pallas_call | solution.py:609
